TPU v7x, 32 devices: a whole 2x2x4 slice. The times are simulated.
32 devices in a mesh: dom: 8 (over y, x, core), feat: 4 (over z).
Axes of the slice: x: 2, y: 2, z: 4, core: 2. Of those that a mesh axis runs over, the one named last changes fastest.
Arguments:
- features: bfloat16 [128, 65536], P('feat', 'dom'), may hold values from -6 to 6
- w1_self: bfloat16 [128, 256], replicated, may hold values from -0.5 to 0.5
- w1_neigh: bfloat16 [128, 256], replicated, may hold values from -0.5 to 0.5
- b1: float32 [256], replicated, may hold values from -3 to 3
- w2_self: bfloat16 [256, 256], replicated, may hold values from -0.375 to 0.375
- w2_neigh: bfloat16 [256, 256], replicated, may hold values from -0.046875 to 0.046875
- b2: float32 [256], replicated, may hold values from -3 to 3
- col_tiles: int32 [512, 32], P(('dom', 'feat')), may hold values from -1 to 511, as said below
- edge_weights: bfloat16 [512, 32, 128, 128], P(('dom', 'feat')), may hold values from 0 to 4, as said below
- cotangent: bfloat16 [65536, 256], P(('dom', 'feat')), may hold values from -0.0625 to 0.0625
Outputs:
- embedding: bfloat16 [65536, 256], P(('dom', 'feat'))
- grad_w2_self: float32 [256, 256], replicated
- grad_w2_neigh: float32 [256, 256], replicated
- grad_b2: float32 [256], replicated
Inputs may be any that keep to these rules, and one draw needn't show every extreme that they name: Partition p holds row tiles p * 64 to (p + 1) * 64 - 1. In each row of col_tiles the live entries come first and the rest are -1; at least one entry of a row is live, and some row has all 32 live. A live entry names a tile of the row tile's own partition or of one of the two partitions beside it, the first and last partitions being beside each other. `edge_weights`: zero where two nodes share no edge.
All inputs are finite; a program needn't handle non-finite values.
Results may differ from a plain program's by a relative error of at most 0.005.
Values may be sent and summed in bfloat16 or wider, within the bound.
A program may use at most 128 MiB of HBM per device.

v0:
```python
import jax
import jax.numpy as jnp
from jax import lax
from jax.sharding import PartitionSpec as P

GROUP = 8


def extended(cells, sides, width):
    for axis, dim in sides:
        count = lax.axis_size(axis)
        head = lax.slice_in_dim(cells, 0, width, axis=dim)
        tail = lax.slice_in_dim(cells, cells.shape[dim] - width, cells.shape[dim], axis=dim)
        cells = jnp.concatenate(
            [
                lax.ppermute(tail, axis, [(i, (i + 1) % count) for i in range(count)]),
                cells,
                lax.ppermute(head, axis, [((i + 1) % count, i) for i in range(count)]),
            ],
            axis=dim,
        )
    return cells


def aggregate(panel, position, occupied, edge_weights, group_turns, with_degree):
    width = panel.shape[1]
    tile_rows = panel.reshape(panel.shape[0] // 128, 128, width)
    row_tiles = position.shape[0]

    def one_group(turn, carry):
        first_slot = turn * GROUP
        slot_where = lax.dynamic_slice_in_dim(position, first_slot, GROUP, 1)
        slot_live = lax.dynamic_slice_in_dim(occupied, first_slot, GROUP, 1)
        edge_block = lax.dynamic_slice_in_dim(edge_weights, first_slot, GROUP, 1)
        adjacency = jnp.where(
            slot_live[:, :, None, None], edge_block, jnp.zeros((), edge_block.dtype)
        )
        picked = tile_rows[slot_where]
        product = jnp.einsum(
            "rgij,rgjc->ric", adjacency, picked, preferred_element_type=jnp.float32
        )
        if with_degree:
            return (
                carry[0] + product,
                carry[1] + jnp.sum(adjacency.astype(jnp.float32), axis=(1, 3)),
            )
        return carry + product

    zeros_rows = jnp.zeros((row_tiles, 128, width), jnp.float32)
    if with_degree:
        initial = (zeros_rows, jnp.zeros((row_tiles, 128), jnp.float32))
        running, degree = lax.fori_loop(0, group_turns, one_group, initial)
        return (running.reshape(row_tiles * 128, width), degree.reshape(row_tiles * 128))
    running = lax.fori_loop(0, group_turns, one_group, zeros_rows)
    return running.reshape(row_tiles * 128, width)


def panel_of(values):
    partition = lax.all_gather(values, "feat", axis=0, tiled=True)
    return extended(partition, (("dom", 0),), partition.shape[0])


def on_device(
    features, w1_self, w1_neigh, b1, w2_self, w2_neigh, b2, col_tiles, edge_weights, cotangent
):
    feat_count = lax.axis_size("feat")
    dom_count = lax.axis_size("dom")
    contract_first = (((0,), (0,)), ((), ()))
    node_rows = lax.all_to_all(features.T, "feat", split_axis=0, concat_axis=1, tiled=True)
    self_one = jnp.dot(node_rows, w1_self, preferred_element_type=jnp.float32)
    quarter_tiles = col_tiles.shape[0]
    slot_count = col_tiles.shape[1]
    panel_tiles = quarter_tiles * feat_count
    all_tiles = panel_tiles * dom_count
    occupied = col_tiles >= 0
    relative = jnp.mod(col_tiles - (lax.axis_index("dom") - 1) * panel_tiles, all_tiles)
    relative = jnp.where(occupied, relative, 0)
    group_turns = slot_count // GROUP
    summed_one, degree = aggregate(
        panel_of(node_rows), relative, occupied, edge_weights, group_turns, True
    )
    neighbour_one = jnp.dot(
        summed_one, w1_neigh.astype(jnp.float32), precision=lax.Precision.HIGHEST
    )
    inv_root = lax.rsqrt(jnp.maximum(degree, 1.0))[:, None]
    layer_one = jax.nn.relu(self_one + inv_root * neighbour_one + b1).astype(jnp.bfloat16)
    summed_two = aggregate(
        panel_of(layer_one), relative, occupied, edge_weights, group_turns, False
    )
    neighbour_two = (inv_root * summed_two).astype(jnp.bfloat16)
    embedding = (
        jnp.dot(layer_one, w2_self, preferred_element_type=jnp.float32)
        + jnp.dot(neighbour_two, w2_neigh, preferred_element_type=jnp.float32)
        + b2
    ).astype(jnp.bfloat16)
    local_self = lax.dot_general(
        layer_one, cotangent, contract_first, preferred_element_type=jnp.float32
    )
    local_neigh = lax.dot_general(
        neighbour_two, cotangent, contract_first, preferred_element_type=jnp.float32
    )
    local_bias = jnp.sum(cotangent, axis=0, dtype=jnp.float32)
    grad_self, grad_neigh, grad_bias = lax.psum(
        (local_self, local_neigh, local_bias), ("dom", "feat")
    )
    return (embedding, grad_self, grad_neigh, grad_bias)


def solution(mesh):
    placed = (
        P("feat", "dom"),
        P(),
        P(),
        P(),
        P(),
        P(),
        P(),
        P(("dom", "feat"), None),
        P(("dom", "feat"), None, None, None),
        P(("dom", "feat"), None),
    )
    return jax.shard_map(
        on_device,
        mesh=mesh,
        in_specs=placed,
        out_specs=(P(("dom", "feat"), None), P(), P(), P()),
        check_vma=False,
    )
```

profile of v0, /device:TPU:1, one launch (start us, length us, event | category | flops | bytes accessed | tf_op | source)
XLA Modules:
  0.0 653.5 jit_solution(8170506284906998908)
XLA Ops:
  8.3 19.0 %all_to_all.19 = bf16[4,2048,32]{1,2,0:T(8,128)(2,1)} all-to-all(bf16[4,2048,32]{1,2,0:T(8,128)(2,1)S(1)} %bitcast.59), channel_id=1, replica_groups=mesh['dom'=8,'feat'=4] {'feat'}, dimensions={0} | all-to-all | bytes 1048576 | tf_op jit(solution)/shard_map/all_to_all | solution.py:69
  27.4 46.3 %all-gather.3.cloned.1.call-done = bf16[8192,128]{0,1:T(8,128)(2,1)} async-done(((bf16[2048,128]{0,1:T(8,128)(2,1)}), bf16[8192,128]{0,1:T(8,128)(2,1)}) %all-gather.3.cloned.1.call-update) | async-done | bytes 2097168 | tf_op jit(solution)/shard_map/all_gather | solution.py:59
  79.7 39.7 %collective-permute-done = bf16[8192,128]{0,1:T(8,128)(2,1)S(1)} collective-permute-done((bf16[8192,128]{0,1:T(8,128)(2,1)}, bf16[8192,128]{0,1:T(8,128)(2,1)S(1)}, u32[]{:S(2)}, u32[]{:S(2)}) %collective-permute-start) | collective-permute-done | bytes 2097184 | tf_op jit(solution)/shard_map/ppermute | solution.py:16
  119.4 3.4 collective-permute-done.1
  122.8 5.3 pad_maximum_fusion.1
  128.1 8.7 %copy.22 = bf16[24576,128]{1,0:T(8,128)(2,1)} copy(bf16[24576,128]{0,1:T(8,128)(2,1)} %pad_maximum_fusion.1) | data formatting | bytes 12582912
  136.8 56.8 %while.30 = (s32[]{:T(128)}, f32[16,128,128]{2,1,0:T(8,128)S(1)}, f32[16,128]{1,0:T(8,128)S(1)}, pred[16,32]{1,0:T(8,128)(4,1)S(1)}, bf16[16,32,128,128]{3,2,1,0...) while((s32[]{:T(128)}, f32[16,128,128]{2,1,0:T(8,128)S(1)}, ...), condition=%wide.region_2.3_spmd.clone, body=%wide.region_0.2_spmd.clone.sunk | while | flops 545787264 | bytes 23109300 | solution.py:52
  137.0 5.8 gather_fusion
  142.9 4.8 fusion.47
  147.7 3.2 convert_reduce_fusion.3
  151.2 5.8 gather_fusion
  157.1 4.8 fusion.47
  161.9 3.2 convert_reduce_fusion.3
  165.4 5.8 gather_fusion
  171.2 4.8 fusion.47
  176.1 3.2 convert_reduce_fusion.3
  179.6 5.8 gather_fusion
  185.4 4.8 fusion.47
  193.6 3.7 fusion.19
  197.4 78.2 %all-gather.5.cloned.1.call-done = bf16[8192,256]{1,0:T(8,128)(2,1)} async-done(((bf16[2048,256]{1,0:T(8,128)(2,1)}), bf16[8192,256]{1,0:T(8,128)(2,1)}) %all-gather.5.cloned.1.call-update) | async-done | bytes 4194320 | tf_op jit(solution)/shard_map/all_gather | solution.py:59
  277.6 122.8 %psum.23 = f32[256]{0:T(256)} all-reduce(f32[256]{0:T(256)S(1)} %convert_reduce_fusion.1), channel_id=1, replica_groups=mesh['dom'=8,'feat'=4] {'dom','feat'}, use_global_device_ids=true, to_apply=%region_8.9 | all-reduce | flops 256 | bytes 2048 | tf_op jit(solution)/shard_map/psum | solution.py:103
  404.7 30.3 %pad_maximum_fusion = bf16[24576,256]{1,0:T(8,128)(2,1)} fusion(bf16[8192,256]{1,0:T(8,128)(2,1)} %collective-permute-done.3, bf16[8192,256]{1,0:T(8,128)(2,1)S(1)} %copy-done.4, bf16[8192,256]{1,0:T(8,128)(2,1)} %collective-permute-done.2), kind=kLoop, calls=%fused_computation.25 | loop fusion | flops 37748736 | bytes 25165824 | tf_op jit(solution)/shard_map/concatenate | solution.py:14
  435.1 75.8 %while.31 = (s32[]{:T(128)}, f32[16,128,256]{2,1,0:T(8,128)}, pred[16,32]{1,0:T(8,128)(4,1)S(1)}, bf16[16,32,128,128]{3,2,1,0:T(8,128)(2,1)}, s32[16,32]{1,0:T(8...) while((s32[]{:T(128)}, f32[16,128,256]{2,1,0:T(8,128)}, ...), condition=%wide.region_4.5_spmd.clone, body=%wide.region_3.4_spmd.clone.sunk | while | flops 1076888960 | bytes 33562152 | solution.py:54
  435.3 11.1 %gather_fusion.1 = bf16[128,128,256]{2,1,0:T(8,128)(2,1)} fusion(bf16[192,128,256]{2,1,0:T(8,128)(2,1)} %get-tuple-element.473, s32[1024]{0:T(1024)S(1)} %pad_clamp_fusion.5), kind=kCustom, calls=%fused_computation.1.clone.clone.1 | custom fusion | bytes 16777728 | tf_op jit(solution)/shard_map/while/body/eval_jaxpr/gather | solution.py:38
  446.4 7.3 %bitcast_add_fusion.2 = f32[16,128,256]{2,1,0:T(8,128)} fusion(f32[16,128,256]{2,1,0:T(8,128)} %get-tuple-element.459, bf16[16,8,128,256]{3,2,1,0:T(8,128)(2,1)} %bitcast.54, bf16[16,32,128,128]{3,2,1,0:T(8,128)(2,1)} %get-tuple-element.471, s32[]{:T(128)S(6)} %select_n.97, pred[16,8]{1,0:T(8,128)(4,1)S(1)} %constant_dynamic-slice_fusion.5, ...), kind=kOutput, calls=%fused_computation.18.clone.1 | convolution fusion | flops 1076887552 | bytes 16777348 | tf_op jit(solution)/shard_map/while/body/eval_jaxpr/rgij,rgjc->ric/dot_general | solution.py:39
  453.9 11.0 %gather_fusion.1 = bf16[128,128,256]{2,1,0:T(8,128)(2,1)} fusion(bf16[192,128,256]{2,1,0:T(8,128)(2,1)} %get-tuple-element.473, s32[1024]{0:T(1024)S(1)} %pad_clamp_fusion.5), kind=kCustom, calls=%fused_computation.1.clone.clone.1 | custom fusion | bytes 16777728 | tf_op jit(solution)/shard_map/while/body/eval_jaxpr/gather | solution.py:38
  465.0 7.9 %bitcast_add_fusion.2 = f32[16,128,256]{2,1,0:T(8,128)} fusion(f32[16,128,256]{2,1,0:T(8,128)} %get-tuple-element.459, bf16[16,8,128,256]{3,2,1,0:T(8,128)(2,1)} %bitcast.54, bf16[16,32,128,128]{3,2,1,0:T(8,128)(2,1)} %get-tuple-element.471, s32[]{:T(128)S(6)} %select_n.97, pred[16,8]{1,0:T(8,128)(4,1)S(1)} %constant_dynamic-slice_fusion.5, ...), kind=kOutput, calls=%fused_computation.18.clone.1 | convolution fusion | flops 1076887552 | bytes 16777348 | tf_op jit(solution)/shard_map/while/body/eval_jaxpr/rgij,rgjc->ric/dot_general | solution.py:39
  473.1 10.8 %gather_fusion.1 = bf16[128,128,256]{2,1,0:T(8,128)(2,1)} fusion(bf16[192,128,256]{2,1,0:T(8,128)(2,1)} %get-tuple-element.473, s32[1024]{0:T(1024)S(1)} %pad_clamp_fusion.5), kind=kCustom, calls=%fused_computation.1.clone.clone.1 | custom fusion | bytes 16777728 | tf_op jit(solution)/shard_map/while/body/eval_jaxpr/gather | solution.py:38
  484.0 7.9 %bitcast_add_fusion.2 = f32[16,128,256]{2,1,0:T(8,128)} fusion(f32[16,128,256]{2,1,0:T(8,128)} %get-tuple-element.459, bf16[16,8,128,256]{3,2,1,0:T(8,128)(2,1)} %bitcast.54, bf16[16,32,128,128]{3,2,1,0:T(8,128)(2,1)} %get-tuple-element.471, s32[]{:T(128)S(6)} %select_n.97, pred[16,8]{1,0:T(8,128)(4,1)S(1)} %constant_dynamic-slice_fusion.5, ...), kind=kOutput, calls=%fused_computation.18.clone.1 | convolution fusion | flops 1076887552 | bytes 16777348 | tf_op jit(solution)/shard_map/while/body/eval_jaxpr/rgij,rgjc->ric/dot_general | solution.py:39
  492.1 10.8 %gather_fusion.1 = bf16[128,128,256]{2,1,0:T(8,128)(2,1)} fusion(bf16[192,128,256]{2,1,0:T(8,128)(2,1)} %get-tuple-element.473, s32[1024]{0:T(1024)S(1)} %pad_clamp_fusion.5), kind=kCustom, calls=%fused_computation.1.clone.clone.1 | custom fusion | bytes 16777728 | tf_op jit(solution)/shard_map/while/body/eval_jaxpr/gather | solution.py:38
  502.9 7.9 %bitcast_add_fusion.2 = f32[16,128,256]{2,1,0:T(8,128)} fusion(f32[16,128,256]{2,1,0:T(8,128)} %get-tuple-element.459, bf16[16,8,128,256]{3,2,1,0:T(8,128)(2,1)} %bitcast.54, bf16[16,32,128,128]{3,2,1,0:T(8,128)(2,1)} %get-tuple-element.471, s32[]{:T(128)S(6)} %select_n.97, pred[16,8]{1,0:T(8,128)(4,1)S(1)} %constant_dynamic-slice_fusion.5, ...), kind=kOutput, calls=%fused_computation.18.clone.1 | convolution fusion | flops 1076887552 | bytes 16777348 | tf_op jit(solution)/shard_map/while/body/eval_jaxpr/rgij,rgjc->ric/dot_general | solution.py:39
  517.1 126.6 %all-reduce.3.cloned.1.call-done = (f32[256,256]{1,0:T(8,128)}, f32[256,256]{1,0:T(8,128)}) async-done(((f32[256,256]{1,0:T(8,128)}, f32[256,256]{1,0:T(8,128)}), (f32[256,256]{1,0:T(8,128)}, f32[256,256]{1,0:T(8,128)})) %all-reduce.3.cloned.1.call-update) | async-done | bytes 524304 | tf_op jit(solution)/shard_map/psum | solution.py:103
  (83 shorter events, 28.4 us)
Async XLA Ops:
  7.2 395.8 %copy-start = (bf16[256,256]{1,0:T(8,128)(2,1)S(1)}, bf16[256,256]{1,0:T(8,128)(2,1)}, u32[]{:S(2)}) copy-start(bf16[256,256]{1,0:T(8,128)(2,1)} %param.18) | copy-start | bytes 393220
  7.2 66.4 %all-gather.3.cloned.1.call-start = ((), (), s32[]{:S(2)}) async-start(), calls=%async_computation.1 | async-start | bytes 2621440 | tf_op jit(solution)/shard_map/all_gather | solution.py:59
  27.3 248.2 %all-gather.5.cloned.1.call-start = ((), (), s32[]{:S(2)}) async-start(), calls=%async_computation.2 | async-start | bytes 5242880 | tf_op jit(solution)/shard_map/all_gather | solution.py:59
  73.6 45.7 %collective-permute-start = (bf16[8192,128]{0,1:T(8,128)(2,1)}, bf16[8192,128]{0,1:T(8,128)(2,1)S(1)}, u32[]{:S(2)}, u32[]{:S(2)}) collective-permute-start(bf16[8192,128]{0,1:T(8,128)(2,1)} %all-gather.3.cloned.1.call-done), channel_id=1, source_target_pairs={{0,4},{4,8},{8,12},{12,16},{16,20},{20,24},{24,28},{28,0},{1,5},{5... | collective-permute-start | bytes 6291464 | tf_op jit(solution)/shard_map/ppermute | solution.py:16
  75.4 47.4 %collective-permute-start.1 = (bf16[8192,128]{0,1:T(8,128)(2,1)}, bf16[8192,128]{0,1:T(8,128)(2,1)}, u32[]{:S(2)}, u32[]{:S(2)}) collective-permute-start(bf16[8192,128]{0,1:T(8,128)(2,1)} %all-gather.3.cloned.1.call-done), channel_id=1, source_target_pairs={{4,0},{8,4},{12,8},{16,12},{20,16},{24,20},{28,24},{0,28},{5,1},{9... | collective-permute-start | bytes 6291464 | tf_op jit(solution)/shard_map/ppermute | solution.py:18
  136.8 56.8 %copy-start.6 = (bf16[128,256]{1,0:T(8,128)(2,1)S(1)}, bf16[128,256]{1,0:T(8,128)(2,1)}, u32[]{:S(2)}) copy-start(bf16[128,256]{1,0:T(8,128)(2,1)} %param.16) | copy-start | bytes 196612
  136.8 56.8 %copy-start.7 = (f32[256]{0:T(256)S(1)}, f32[256]{0:T(256)}, u32[]{:S(2)}) copy-start(f32[256]{0:T(256)} %param.17) | copy-start | bytes 3076
  193.5 83.7 %copy-start.3 = (bf16[2048,256]{1,0:T(8,128)(2,1)S(1)}, bf16[2048,256]{1,0:T(8,128)(2,1)}, u32[]{:S(2)}) copy-start(bf16[2048,256]{1,0:T(8,128)(2,1)} %param.23) | copy-start | bytes 3145732
  197.3 205.7 %copy-start.2 = (bf16[2048,256]{1,0:T(8,128)(2,1)S(1)}, bf16[2048,256]{1,0:T(8,128)(2,1)}, u32[]{:S(2)}) copy-start(bf16[2048,256]{1,0:T(8,128)(2,1)} %fusion.19) | copy-start | bytes 3145732
  197.3 446.3 %all-reduce.3.cloned.1.call-start = ((), (), s32[]{:S(2)}) async-start(), calls=%async_computation.3 | async-start | bytes 1048576 | tf_op jit(solution)/shard_map/psum | solution.py:103
  275.5 129.2 %collective-permute-start.2 = (bf16[8192,256]{1,0:T(8,128)(2,1)}, bf16[8192,256]{1,0:T(8,128)(2,1)}, u32[]{:S(2)}, u32[]{:S(2)}) collective-permute-start(bf16[8192,256]{1,0:T(8,128)(2,1)} %all-gather.5.cloned.1.call-done), channel_id=1, source_target_pairs={{0,4},{4,8},{8,12},{12,16},{16,20},{20,24},{24,28},{28,0},{1,5},{5... | collective-permute-start | bytes 12582920 | tf_op jit(solution)/shard_map/ppermute | solution.py:16
  277.3 127.4 %collective-permute-start.3 = (bf16[8192,256]{1,0:T(8,128)(2,1)}, bf16[8192,256]{1,0:T(8,128)(2,1)}, u32[]{:S(2)}, u32[]{:S(2)}) collective-permute-start(bf16[8192,256]{1,0:T(8,128)(2,1)} %all-gather.5.cloned.1.call-done), channel_id=1, source_target_pairs={{4,0},{8,4},{12,8},{16,12},{20,16},{24,20},{28,24},{0,28},{5,1},{9... | collective-permute-start | bytes 12582920 | tf_op jit(solution)/shard_map/ppermute | solution.py:18
  400.4 4.3 copy-start.4
  510.9 3.2 copy-start.5
  510.9 3.2 copy-start.8
  510.9 136.1 %copy-start.1 = (bf16[256,256]{1,0:T(8,128)(2,1)S(1)}, bf16[256,256]{1,0:T(8,128)(2,1)}, u32[]{:S(2)}) copy-start(bf16[256,256]{1,0:T(8,128)(2,1)} %param.18) | copy-start | bytes 393220
Sparse Core Ops, SparseCore 0:
  27.4 46.1 all-gather.2
  197.4 78.0 all-gather.4
  514.2 129.4 all-reduce.2
where the time goes:
time: 656 us; the launch traced here: 654 us
  waiting for transfers between devices  294 us (45%)
  blocking collectives  142 us (22%)
  local copies, waits for them, and re-layouts  81.3 us (12%)
  matrix products  65.5 us (10%)
  other arithmetic  53 us (8%)
  between operations  13.8 us (2%)
    psum x1, waiting for transfers between devices, on_device(): lax.psum((local_self, local_neigh, local_bias), ('dom', 'feat'))  127 us
    all_gather x2, waiting for transfers between devices, panel_of(): partition = lax.all_gather(values, 'feat', axis=0, tiled=True)  124 us
    psum x1, blocking collectives, on_device(): lax.psum((local_self, local_neigh, local_bias), ('dom', 'feat'))  123 us
    gather x8, local copies, waits for them, and re-layouts, one_group(): picked = tile_rows[slot_where]  66.9 us
    dot_general x8, matrix products, one_group(): jnp.einsum('rgij,rgjc->ric', adjacency, picked, preferred_element_type=jn...  50.4 us
    ppermute x2, waiting for transfers between devices, extended(): lax.ppermute(tail, axis, [(i, (i + 1) % count) for i in range(count)])  39.7 us
    concatenate x2, other arithmetic, extended(): jnp.concatenate([lax.ppermute(tail, axis, [(i, (i + 1) % count) for i in...  35.6 us
    all_to_all x1, blocking collectives, on_device(): lax.all_to_all(features.T, 'feat', split_axis=0, concat_axis=1, tiled=True)  19 us
  transfers between devices with their start and end apart: 7, of which 5 were waited for; matrix products, arithmetic and copies ran while one was open for 2% of the time, Pallas kernels for 0%

commit v1 on v0

v1 whole, which is shorter than its diff:
```python
import functools

import jax
import jax.numpy as jnp
from jax import lax
from jax.experimental import pallas as pl
from jax.experimental.pallas import tpu as pltpu
from jax.sharding import PartitionSpec as P

MESH = pl.DeviceIdType.MESH
GROUP = 8
VMEM_LIMIT = 56 * 1024 * 1024


def gather_kernel(n_dom, n_feat, pieces, x_ref, out_ref, own_sem, send_sem, recv_sem):
    dom, feat = lax.axis_index("dom"), lax.axis_index("feat")
    right, left = lax.rem(dom + 1, n_dom), lax.rem(dom + n_dom - 1, n_dom)
    above, below = lax.rem(feat + 1, n_feat), lax.rem(feat + n_feat - 1, n_feat)
    size = x_ref.shape[0] // pieces

    barrier = pltpu.get_barrier_semaphore()
    for where in ((left, feat), (right, feat), (dom, above), (dom, below)):
        pl.semaphore_signal(barrier, inc=1, device_id=where, device_id_type=MESH)
    pl.semaphore_wait(barrier, 4)

    def rows(piece):
        return pl.ds(piece * size, size)

    def copy(way, block, piece, own):
        slot, target = (
            (1, (dom, above)),
            (1, (dom, below)),
            (2, (left, feat)),
            (0, (right, feat)),
        )[way]
        source = x_ref if own else out_ref.at[1, block]
        return pltpu.make_async_remote_copy(
            src_ref=source.at[rows(piece)],
            dst_ref=out_ref.at[slot, block, rows(piece)],
            send_sem=send_sem.at[way, block, piece],
            recv_sem=recv_sem.at[slot, block, piece],
            device_id=target,
            device_id_type=MESH,
        )

    def arrival(slot, block, piece):
        part = out_ref.at[slot, block, rows(piece)]
        return pltpu.make_async_copy(part, part, recv_sem.at[slot, block, piece])

    keep = pltpu.make_async_copy(x_ref, out_ref.at[1, feat], own_sem)
    for piece in range(pieces):
        for way, there in ((0, feat < n_feat - 1), (1, feat > 0)):

            @pl.when(there)
            def _():
                copy(way, feat, piece, True).start()

        copy(2, feat, piece, True).start()
        copy(3, feat, piece, True).start()
    keep.start()

    for step in range(1, n_feat):
        for piece in range(pieces):
            for way, block, there, onward in (
                (0, feat - step, feat >= step, feat < n_feat - 1),
                (1, feat + step, feat + step < n_feat, feat > 0),
            ):

                @pl.when(there)
                def _():
                    arrival(1, block, piece).wait()

                    @pl.when(onward)
                    def _():
                        copy(way, block, piece, False).start()

                    copy(2, block, piece, False).start()
                    copy(3, block, piece, False).start()

    keep.wait()
    for piece in range(pieces):
        for way, there in ((0, feat < n_feat - 1), (1, feat > 0)):

            @pl.when(there)
            def _():
                copy(way, feat, piece, True).wait_send()

        copy(2, feat, piece, True).wait_send()
        copy(3, feat, piece, True).wait_send()
        for step in range(1, n_feat):
            for way, block, there, onward in (
                (0, feat - step, feat >= step, feat < n_feat - 1),
                (1, feat + step, feat + step < n_feat, feat > 0),
            ):

                @pl.when(there)
                def _():
                    @pl.when(onward)
                    def _():
                        copy(way, block, piece, False).wait_send()

                    copy(2, block, piece, False).wait_send()
                    copy(3, block, piece, False).wait_send()

        for block in range(n_feat):
            arrival(0, block, piece).wait()
            arrival(2, block, piece).wait()


def gather(block, n_dom, n_feat, pieces, collective_id, name):
    return pl.pallas_call(
        functools.partial(gather_kernel, n_dom, n_feat, pieces),
        out_shape=jax.ShapeDtypeStruct((3, n_feat) + block.shape, block.dtype),
        in_specs=[pl.BlockSpec(memory_space=pl.ANY)],
        out_specs=pl.BlockSpec(memory_space=pl.ANY),
        scratch_shapes=[
            pltpu.SemaphoreType.DMA,
            pltpu.SemaphoreType.DMA((4, n_feat, pieces)),
            pltpu.SemaphoreType.DMA((3, n_feat, pieces)),
        ],
        compiler_params=pltpu.CompilerParams(
            collective_id=collective_id, has_side_effects=True
        ),
        name=name,
    )(block)


def live_group(edge_ref, tile, first, count):
    parts = []
    for lane in range(GROUP):
        weights = edge_ref[tile, first + lane]
        parts.append(jnp.where(first + lane < count, weights, jnp.zeros_like(weights)))
    return parts


def first_kernel(
    panel_tiles, where_ref, count_ref, feat_ref, panel_ref, edge_ref, ws_ref, wn_ref, b_ref,
    layer_ref, root_ref,
):
    tile = pl.program_id(0)
    count = count_ref[tile]

    def one_group(turn, carry):
        total, degree = carry
        first = turn * GROUP
        parts = live_group(edge_ref, 0, first, count)
        picked = []
        for lane in range(GROUP):
            at = where_ref[tile, first + lane]
            column = pl.multiple_of(lax.rem(at, panel_tiles) * 128, 128)
            picked.append(panel_ref[lax.div(at, panel_tiles), :, pl.ds(column, 128)])
        total += lax.dot_general(
            jnp.concatenate(parts, axis=1),
            jnp.concatenate(picked, axis=1),
            (((1,), (1,)), ((), ())),
            preferred_element_type=jnp.float32,
        )
        for part in parts:
            degree += part.astype(jnp.float32)
        return total, degree

    zeros = jnp.zeros((128, 128), jnp.float32)
    summed, degree = lax.fori_loop(0, pl.cdiv(count, GROUP), one_group, (zeros, zeros))
    degree = jnp.sum(degree, axis=1, keepdims=True)
    inv_root = lax.rsqrt(jnp.maximum(degree, 1.0))
    neighbour = jnp.zeros(layer_ref.shape, jnp.float32)
    rest = summed
    for _ in range(3):
        piece = rest.astype(jnp.bfloat16)
        rest = rest - piece.astype(jnp.float32)
        neighbour += jnp.dot(piece, wn_ref[...], preferred_element_type=jnp.float32)
    own = pl.multiple_of((feat_ref[0] * pl.num_programs(0) + tile) * 128, 128)
    self_one = lax.dot_general(
        panel_ref[1, :, pl.ds(own, 128)],
        ws_ref[...],
        (((0,), (0,)), ((), ())),
        preferred_element_type=jnp.float32,
    )
    layer = self_one + inv_root * neighbour + b_ref[...]
    layer_ref[...] = jnp.maximum(layer, 0.0).astype(layer_ref.dtype)
    root_ref[...] = jnp.broadcast_to(inv_root, root_ref.shape)


def second_kernel(
    where_ref, count_ref, panel_ref, edge_ref, layer_ref, root_ref, cot_ref, ws_ref, wn_ref,
    b_ref, emb_ref, grad_ref, bias_ref,
):
    tile = pl.program_id(0)
    count = count_ref[tile]
    hidden = layer_ref.shape[1]

    def one_group(turn, total):
        first = turn * GROUP
        parts = live_group(edge_ref, 0, first, count)
        picked = [panel_ref[where_ref[tile, first + lane]] for lane in range(GROUP)]
        return total + jnp.dot(
            jnp.concatenate(parts, axis=1),
            jnp.concatenate(picked, axis=0),
            preferred_element_type=jnp.float32,
        )

    zeros = jnp.zeros((128, hidden), jnp.float32)
    summed = lax.fori_loop(0, pl.cdiv(count, GROUP), one_group, zeros)
    neighbour = (root_ref[:, :1] * summed).astype(jnp.bfloat16)
    layer = layer_ref[...]
    embedding = (
        jnp.dot(layer, ws_ref[...], preferred_element_type=jnp.float32)
        + jnp.dot(neighbour, wn_ref[...], preferred_element_type=jnp.float32)
        + b_ref[...]
    )
    emb_ref[...] = embedding.astype(emb_ref.dtype)
    cotangent = cot_ref[...]

    @pl.when(tile == 0)
    def _():
        grad_ref[...] = jnp.zeros_like(grad_ref)
        bias_ref[...] = jnp.zeros_like(bias_ref)

    grad_ref[...] += lax.dot_general(
        jnp.concatenate([layer, neighbour], axis=1),
        cotangent,
        (((0,), (0,)), ((), ())),
        preferred_element_type=jnp.float32,
    )
    bias_ref[...] += jnp.sum(
        cotangent.astype(jnp.float32).reshape(16, 8, cotangent.shape[1]), axis=0
    )


def reduce_kernel(
    n_dom, n_feat, g_ref, b_ref, out_ref, bias_ref,
    by_dom, bias_dom, by_feat, bias_feat, send_sem, recv_sem,
):
    dom, feat = lax.axis_index("dom"), lax.axis_index("feat")
    share = g_ref.shape[0] // n_dom

    def dom_at(step):
        return lax.rem(dom + step, n_dom)

    def feat_at(step):
        return lax.rem(feat + step, n_feat)

    def rows(index):
        return pl.ds(pl.multiple_of(index * share, share), share)

    def copy(kind, source, target, step, device_id):
        return pltpu.make_async_remote_copy(
            src_ref=source,
            dst_ref=target,
            send_sem=send_sem.at[kind, step],
            recv_sem=recv_sem.at[kind, step],
            device_id=device_id,
            device_id_type=MESH,
        )

    barrier = pltpu.get_barrier_semaphore()
    for step in range(1, n_dom):
        pl.semaphore_signal(
            barrier, inc=1, device_id=(dom_at(step), feat), device_id_type=MESH
        )
    for step in range(1, n_feat):
        pl.semaphore_signal(
            barrier, inc=1, device_id=(dom, feat_at(step)), device_id_type=MESH
        )
    pl.semaphore_wait(barrier, n_dom + n_feat - 2)

    scatter = []
    for step in range(1, n_dom):
        to = (dom_at(step), feat)
        scatter.append(copy(0, g_ref.at[rows(dom_at(step))], by_dom.at[dom], step, to))
        scatter.append(copy(1, b_ref, bias_dom.at[dom], step, to))
    for each in scatter:
        each.start()
    by_dom[dom] = g_ref[rows(dom), :]
    bias_dom[dom] = b_ref[...]
    for each in scatter:
        each.wait()
    by_feat[feat] = functools.reduce(lambda a, b: a + b, [by_dom[i] for i in range(n_dom)])
    bias_feat[feat] = functools.reduce(
        lambda a, b: a + b, [bias_dom[i] for i in range(n_dom)]
    )

    across = []
    for step in range(1, n_feat):
        to = (dom, feat_at(step))
        across.append(copy(2, by_feat.at[feat], by_feat.at[feat], step, to))
        across.append(copy(3, bias_feat.at[feat], bias_feat.at[feat], step, to))
    for each in across:
        each.start()
    for each in across:
        each.wait()
    out_ref[rows(dom), :] = functools.reduce(
        lambda a, b: a + b, [by_feat[i] for i in range(n_feat)]
    )
    bias_ref[...] = functools.reduce(lambda a, b: a + b, [bias_feat[i] for i in range(n_feat)])

    spread = [
        copy(4, out_ref.at[rows(dom)], out_ref.at[rows(dom)], step, (dom_at(step), feat))
        for step in range(1, n_dom)
    ]
    for each in spread:
        each.start()
    for each in spread:
        each.wait()


def reduce_all(grads, bias, n_dom, n_feat):
    share = grads.shape[0] // n_dom
    width = grads.shape[1]
    steps = max(n_dom, n_feat)
    whole = pl.BlockSpec(memory_space=pltpu.VMEM)
    return pl.pallas_call(
        functools.partial(reduce_kernel, n_dom, n_feat),
        out_shape=(
            jax.ShapeDtypeStruct(grads.shape, jnp.float32),
            jax.ShapeDtypeStruct(bias.shape, jnp.float32),
        ),
        in_specs=[whole] * 2,
        out_specs=(whole, whole),
        scratch_shapes=[
            pltpu.VMEM((n_dom, share, width), jnp.float32),
            pltpu.VMEM((n_dom,) + bias.shape, jnp.float32),
            pltpu.VMEM((n_feat, share, width), jnp.float32),
            pltpu.VMEM((n_feat,) + bias.shape, jnp.float32),
            pltpu.SemaphoreType.DMA((5, steps)),
            pltpu.SemaphoreType.DMA((5, steps)),
        ],
        compiler_params=pltpu.CompilerParams(
            collective_id=2, has_side_effects=True, vmem_limit_bytes=VMEM_LIMIT
        ),
        name="reduce_all",
    )(grads, bias)


def on_device(
    features, w1_self, w1_neigh, b1, w2_self, w2_neigh, b2, col_tiles, edge_weights, cotangent
):
    n_feat = lax.axis_size("feat")
    n_dom = lax.axis_size("dom")
    row_tiles, slots = col_tiles.shape
    panel_tiles = row_tiles * n_feat
    all_tiles = panel_tiles * n_dom
    inputs, hidden = w1_self.shape
    occupied = col_tiles >= 0
    relative = jnp.mod(col_tiles - (lax.axis_index("dom") - 1) * panel_tiles, all_tiles)
    relative = jnp.where(occupied, relative, 0)
    counts = jnp.sum(occupied.astype(jnp.int32), axis=1)
    feat = jnp.full((1,), lax.axis_index("feat"), jnp.int32)

    def fixed(*shape):
        return pl.BlockSpec(
            shape, lambda r, *_: (0,) * len(shape), pipeline_mode=pl.Buffered(1)
        )

    def by_tile(width):
        return pl.BlockSpec((128, width), lambda r, *_: (r, 0))

    edges = pl.BlockSpec((1, slots, 128, 128), lambda r, *_: (r, 0, 0, 0))
    rows = row_tiles * 128

    panel_one = gather(features, n_dom, n_feat, 2, 0, "gather_features")
    panel_one = panel_one.reshape(3, inputs, panel_tiles * 128)
    layer_one, inv_root = pl.pallas_call(
        functools.partial(first_kernel, panel_tiles),
        grid_spec=pltpu.PrefetchScalarGridSpec(
            num_scalar_prefetch=3,
            grid=(row_tiles,),
            in_specs=[
                fixed(3, inputs, panel_tiles * 128),
                edges,
                fixed(inputs, hidden),
                fixed(inputs, hidden),
                fixed(1, hidden),
            ],
            out_specs=(by_tile(hidden), by_tile(128)),
        ),
        out_shape=(
            jax.ShapeDtypeStruct((rows, hidden), jnp.bfloat16),
            jax.ShapeDtypeStruct((rows, 128), jnp.float32),
        ),
        compiler_params=pltpu.CompilerParams(vmem_limit_bytes=VMEM_LIMIT),
        name="first_layer",
    )(relative, counts, feat, panel_one, edge_weights, w1_self, w1_neigh, b1[None])

    panel_two = gather(layer_one, n_dom, n_feat, 4, 1, "gather_layer_one")
    panel_two = panel_two.reshape(3 * panel_tiles, 128, hidden)
    embedding, grads, bias = pl.pallas_call(
        second_kernel,
        grid_spec=pltpu.PrefetchScalarGridSpec(
            num_scalar_prefetch=2,
            grid=(row_tiles,),
            in_specs=[
                fixed(3 * panel_tiles, 128, hidden),
                edges,
                by_tile(hidden),
                by_tile(128),
                by_tile(hidden),
                fixed(hidden, hidden),
                fixed(hidden, hidden),
                fixed(1, hidden),
            ],
            out_specs=(
                by_tile(hidden),
                pl.BlockSpec((2 * hidden, hidden), lambda r, *_: (0, 0)),
                pl.BlockSpec((8, hidden), lambda r, *_: (0, 0)),
            ),
        ),
        out_shape=(
            jax.ShapeDtypeStruct((rows, hidden), jnp.bfloat16),
            jax.ShapeDtypeStruct((2 * hidden, hidden), jnp.float32),
            jax.ShapeDtypeStruct((8, hidden), jnp.float32),
        ),
        compiler_params=pltpu.CompilerParams(vmem_limit_bytes=VMEM_LIMIT),
        name="second_layer",
    )(
        relative, counts, panel_two, edge_weights, layer_one, inv_root, cotangent,
        w2_self, w2_neigh, b2[None],
    )
    grads, bias = reduce_all(grads, bias, n_dom, n_feat)
    return (embedding, grads[:hidden], grads[hidden:], jnp.sum(bias, axis=0))


def solution(mesh):
    placed = (
        P("feat", "dom"),
        P(),
        P(),
        P(),
        P(),
        P(),
        P(),
        P(("dom", "feat"), None),
        P(("dom", "feat"), None, None, None),
        P(("dom", "feat"), None),
    )
    return jax.shard_map(
        on_device,
        mesh=mesh,
        in_specs=placed,
        out_specs=(P(("dom", "feat"), None), P(), P(), P()),
        check_vma=False,
    )
```

time: 656 us -> 229 us (0.35)
  waiting for transfers between devices: 294 us -> 0 us
  Pallas kernels: 0 us -> 227 us
  blocking collectives: 142 us -> 0 us
  local copies, waits for them, and re-layouts: 81.3 us -> 1.85 us
  matrix products: 65.5 us -> 0 us
  other arithmetic: 53 us -> 3.2 us
  between operations: 13.8 us -> 0.67 us
    pallas_call x0 -> x5, Pallas kernels: none -> 227 us  [the longest x2 146 us: gather(): pl.pallas_call(functools.partial(gather_kernel, n_dom, n_feat, pieces), o...]
    psum x1 -> x0, waiting for transfers between devices: 127 us -> none  [on_device(): lax.psum((local_self, local_neigh, local_bias), ('dom', 'feat'))]
    all_gather x2 -> x0, waiting for transfers between devices: 124 us -> none  [panel_of(): partition = lax.all_gather(values, 'feat', axis=0, tiled=True)]
    psum x1 -> x0, blocking collectives: 123 us -> none  [on_device(): lax.psum((local_self, local_neigh, local_bias), ('dom', 'feat'))]
    gather x8 -> x0, local copies, waits for them, and re-layouts: 66.9 us -> none  [one_group(): picked = tile_rows[slot_where]]
    dot_general x14 -> x0, matrix products: 65.5 us -> none  [the longest x8 50.4 us: one_group(): jnp.einsum('rgij,rgjc->ric', adjacency, picked, preferred_element_type=jn...]
    ppermute x4 -> x0, waiting for transfers between devices: 43.2 us -> none  [the longest x2 39.7 us: extended(): lax.ppermute(tail, axis, [(i, (i + 1) % count) for i in range(count)])]
    concatenate x2 -> x0, other arithmetic: 35.6 us -> none  [extended(): jnp.concatenate([lax.ppermute(tail, axis, [(i, (i + 1) % count) for i in...]
  transfers between devices with their start and end apart: 7 -> 0, of which waited for: 5 -> 0; matrix products, arithmetic and copies ran while one was open for 2% -> 0% of each run, Pallas kernels for 0% -> 0%
where the time goes in v1:
time: 229 us; the launch traced here: 233 us
  Pallas kernels  227 us (99%)
  other arithmetic  3.2 us (1%)
    pallas_call x2, Pallas kernels, gather(): pl.pallas_call(functools.partial(gather_kernel, n_dom, n_feat, pieces), o...  146 us
    pallas_call x1, Pallas kernels, on_device(): pl.pallas_call(second_kernel, grid_spec=pltpu.PrefetchScalarGridSpec(num_...  29.8 us
    pallas_call x1, Pallas kernels, reduce_all(): pl.pallas_call(functools.partial(reduce_kernel, n_dom, n_feat), out_shape...  25.8 us
    pallas_call x1, Pallas kernels, on_device(): pl.pallas_call(functools.partial(first_kernel, panel_tiles), grid_spec=pl...  25.3 us

profile of v1, /device:TPU:1, one launch (start us, length us, event | category | flops | bytes accessed | tf_op | source)
XLA Modules:
  0.0 232.8 jit_solution(4485448739885001236)
XLA Ops:
  0.6 1.9 convert_reduce_fusion
  2.6 52.2 %gather_features.1 = bf16[3,4,32,8192]{3,2,1,0:T(8,128)(2,1)} custom-call(bf16[32,8192]{1,0:T(8,128)(2,1)} %x_ref.1), custom_call_target="tpu_custom_call" | custom-call | tf_op jit(solution)/shard_map/gather_features/pallas_call | solution.py:111
  54.8 25.3 %first_layer.1 = (bf16[2048,256]{1,0:T(8,128)(2,1)}, f32[2048,128]{1,0:T(8,128)}) custom-call(s32[16,32]{1,0:T(8,128)} %get-tuple-element.21.where_ref, s32[16]{0:T(128)} %get-tuple-element.20.count_ref, s32[1]{0:T(128)} %bitcast.feat_ref, bf16[3,128,8192]{2,1,0:T(8,128)(2,1)} %bitcast.6, bf16[16,32,128,128]{3,2,1,0:T(8,128)(2,1)} %edge_ref.3, ...), custom_call_target="tpu_custom_call" | custom-call | tf_op jit(solution)/shard_map/first_layer/pallas_call | solution.py:363
  80.1 94.0 %gather_layer_one.1 = bf16[3,4,2048,256]{3,2,1,0:T(8,128)(2,1)} custom-call(bf16[2048,256]{1,0:T(8,128)(2,1)} %get-tuple-element.11.x_ref.layer_ref), custom_call_target="tpu_custom_call" | custom-call | tf_op jit(solution)/shard_map/gather_layer_one/pallas_call | solution.py:111
  174.1 29.8 %second_layer.1 = (bf16[2048,256]{1,0:T(8,128)(2,1)}, f32[512,256]{1,0:T(8,128)}, f32[8,256]{1,0:T(8,128)}) custom-call(s32[16,32]{1,0:T(8,128)} %get-tuple-element.21.where_ref, s32[16]{0:T(128)} %get-tuple-element.20.count_ref, bf16[192,128,256]{2,1,0:T(8,128)(2,1)} %bitcast.5, bf16[16,32,128,128]{3,2,1,0:T(8,128)(2,1)} %edge_ref.3, ...), custom_call_target="tpu_custom_call" | custom-call | tf_op jit(solution)/shard_map/second_layer/pallas_call | solution.py:387
  203.8 25.8 %reduce_all.1 = (f32[512,256]{1,0:T(8,128)}, f32[8,256]{1,0:T(8,128)}) custom-call(f32[512,256]{1,0:T(8,128)} %get-tuple-element.14.g_ref, f32[8,256]{1,0:T(8,128)} %get-tuple-element.15.b_ref), custom_call_target="tpu_custom_call" | custom-call | tf_op jit(solution)/shard_map/reduce_all/pallas_call | solution.py:312
  229.6 1.9 fusion.2
  231.5 1.3 reduce_sum.19

commit v2 on v1

v2 whole, which is shorter than its diff:
```python
import functools

import jax
import jax.numpy as jnp
from jax import lax
from jax.experimental import pallas as pl
from jax.experimental.pallas import tpu as pltpu
from jax.sharding import PartitionSpec as P

MESH = pl.DeviceIdType.MESH
GROUP = 8
PIECES_ONE = 2
PIECES_TWO = 4
VMEM_LIMIT = 56 * 1024 * 1024


def live_group(edge_ref, tile, first, count):
    parts = []
    for lane in range(GROUP):
        weights = edge_ref[tile, first + lane]
        parts.append(jnp.where(first + lane < count, weights, jnp.zeros_like(weights)))
    return parts


def first_kernel(
    n_dom, n_feat, x_ref, where_ref, live_ref, edge_hbm, ws_ref, wn_ref, b_ref,
    out_ref, root_ref,
    panel, tiles_ref, edge_ref, layer_ref, own_sem, edge_sem, send_one, recv_one, send_two, recv_two,
):
    dom, feat = lax.axis_index("dom"), lax.axis_index("feat")
    right, left = lax.rem(dom + 1, n_dom), lax.rem(dom + n_dom - 1, n_dom)
    above, below = lax.rem(feat + 1, n_feat), lax.rem(feat + n_feat - 1, n_feat)
    row_tiles, slots = edge_ref.shape[:2]
    step_tiles = row_tiles // PIECES_TWO

    def edge_copy(piece):
        part = pl.ds(piece * step_tiles, step_tiles)
        return pltpu.make_async_copy(edge_hbm.at[part], edge_ref.at[part], edge_sem.at[piece])

    for piece in range(PIECES_TWO):
        edge_copy(piece).start()

    barrier = pltpu.get_barrier_semaphore()
    for where in ((left, feat), (right, feat), (dom, above), (dom, below)):
        pl.semaphore_signal(barrier, inc=1, device_id=where, device_id_type=MESH)
    pl.semaphore_wait(barrier, 4)

    def gather(block_ref, held_ref, pieces, send_sem, recv_sem):
        size = block_ref.shape[0] // pieces

        def rows(piece):
            return pl.ds(piece * size, size)

        def copy(way, block, piece, own):
            slot, target = (
                (1, (dom, above)),
                (1, (dom, below)),
                (2, (left, feat)),
                (0, (right, feat)),
            )[way]
            source = block_ref if own else held_ref.at[1, block]
            return pltpu.make_async_remote_copy(
                src_ref=source.at[rows(piece)],
                dst_ref=held_ref.at[slot, block, rows(piece)],
                send_sem=send_sem.at[way, block, piece],
                recv_sem=recv_sem.at[slot, block, piece],
                device_id=target,
                device_id_type=MESH,
            )

        def arrival(slot, block, piece):
            part = held_ref.at[slot, block, rows(piece)]
            return pltpu.make_async_copy(part, part, recv_sem.at[slot, block, piece])

        def send_own(piece):
            for way, there in ((0, feat < n_feat - 1), (1, feat > 0)):

                @pl.when(there)
                def _():
                    copy(way, feat, piece, True).start()

            copy(2, feat, piece, True).start()
            copy(3, feat, piece, True).start()

        def streams(step):
            return (
                (0, feat - step, feat >= step, feat < n_feat - 1),
                (1, feat + step, feat + step < n_feat, feat > 0),
            )

        def forward():
            for step in range(1, n_feat):
                for piece in range(pieces):
                    for way, block, there, onward in streams(step):

                        @pl.when(there)
                        def _():
                            arrival(1, block, piece).wait()

                            @pl.when(onward)
                            def _():
                                copy(way, block, piece, False).start()

                            copy(2, block, piece, False).start()
                            copy(3, block, piece, False).start()

        def finish_sends():
            for piece in range(pieces):
                for way, there in ((0, feat < n_feat - 1), (1, feat > 0)):

                    @pl.when(there)
                    def _():
                        copy(way, feat, piece, True).wait_send()

                copy(2, feat, piece, True).wait_send()
                copy(3, feat, piece, True).wait_send()
                for step in range(1, n_feat):
                    for way, block, there, onward in streams(step):

                        @pl.when(there)
                        def _():
                            @pl.when(onward)
                            def _():
                                copy(way, block, piece, False).wait_send()

                            copy(2, block, piece, False).wait_send()
                            copy(3, block, piece, False).wait_send()

        def arrive():
            for piece in range(pieces):
                for block in range(n_feat):
                    arrival(0, block, piece).wait()
                    arrival(2, block, piece).wait()

        return send_own, forward, finish_sends, arrive

    send_own, forward, finish_one, arrive = gather(x_ref, panel, PIECES_ONE, send_one, recv_one)
    keep = pltpu.make_async_copy(x_ref, panel.at[1, feat], own_sem)
    for piece in range(PIECES_ONE):
        send_own(piece)
    keep.start()
    forward()
    keep.wait()
    arrive()

    width = panel.shape[1] * panel.shape[2]
    hidden = layer_ref.shape[1]
    panel_tiles = panel.shape[3] // 128

    tiles_ref[3 * panel_tiles] = jnp.zeros((width, 128), tiles_ref.dtype)

    @pl.loop(0, panel_tiles)
    def _(at):
        column = pl.multiple_of(at * 128, 128)
        for slot in range(3):
            cells = panel[slot, :, :, pl.ds(column, 128)]
            tiles_ref[slot * panel_tiles + at] = cells.reshape(width, 128)

    def two_tiles(pair):
        def one_group(turn, carry):
            done = []
            for half in range(2):
                total, degree = carry[half]
                tile = pair * 2 + half
                first = turn * GROUP
                parts = [edge_ref[tile, first + lane] for lane in range(GROUP)]
                picked = [tiles_ref[where_ref[tile, first + lane]] for lane in range(GROUP)]
                total += lax.dot_general(
                    jnp.concatenate(parts, axis=1),
                    jnp.concatenate(picked, axis=1),
                    (((1,), (1,)), ((), ())),
                    preferred_element_type=jnp.float32,
                )
                for lane, part in enumerate(parts):
                    live = live_ref[pl.ds(tile * slots + first + lane, 1), :]
                    degree += part.astype(jnp.float32) * live
                done.append((total, degree))
            return tuple(done)

        zeros = (jnp.zeros((128, width), jnp.float32), jnp.zeros((128, 128), jnp.float32))
        sums = lax.fori_loop(0, slots // GROUP, one_group, (zeros, zeros))
        rest = jnp.concatenate([total for total, _ in sums], axis=0)
        degree = jnp.sum(
            jnp.concatenate([each for _, each in sums], axis=0), axis=1, keepdims=True
        )
        inv_root = lax.rsqrt(jnp.maximum(degree, 1.0))
        neighbour = jnp.zeros((256, hidden), jnp.float32)
        for _ in range(3):
            piece = rest.astype(jnp.bfloat16)
            rest = rest - piece.astype(jnp.float32)
            neighbour += jnp.dot(piece, wn_ref[...], preferred_element_type=jnp.float32)
        own = pl.multiple_of((feat * row_tiles + pair * 2) * 128, 256)
        self_one = lax.dot_general(
            panel[1, :, :, pl.ds(own, 256)].reshape(width, 256),
            ws_ref[...],
            (((0,), (0,)), ((), ())),
            preferred_element_type=jnp.float32,
        )
        layer = jnp.maximum(self_one + inv_root * neighbour + b_ref[...], 0.0)
        rows = pl.ds(pl.multiple_of(pair * 256, 256), 256)
        layer_ref[rows, :] = layer.astype(layer_ref.dtype)
        root_ref[rows, :] = jnp.broadcast_to(inv_root, (256, 128))

    send_own, forward, finish_two, arrive = gather(
        layer_ref, out_ref, PIECES_TWO, send_two, recv_two
    )
    pairs = step_tiles // 2
    for piece in range(PIECES_TWO):
        edge_copy(piece).wait()
        pl.loop(piece * pairs, (piece + 1) * pairs)(two_tiles)
        send_own(piece)
    keep = pltpu.make_async_copy(layer_ref, out_ref.at[1, feat], own_sem)
    keep.start()
    forward()
    keep.wait()
    finish_one()
    finish_two()
    arrive()


def second_kernel(
    where_ref, count_ref, first_ref, panel_ref, edge_ref, root_ref, cot_ref, ws_ref,
    wn_ref, b_ref, emb_ref, grad_ref, bias_ref,
):
    step = pl.program_id(0)
    hidden = emb_ref.shape[1]
    sums, own = [], []
    for half in range(2):
        tile = step * 2 + half
        count = count_ref[tile]

        def one_group(turn, total):
            first = turn * GROUP
            parts = live_group(edge_ref, half, first, count)
            picked = [panel_ref[where_ref[tile, first + lane]] for lane in range(GROUP)]
            return total + jnp.dot(
                jnp.concatenate(parts, axis=1),
                jnp.concatenate(picked, axis=0),
                preferred_element_type=jnp.float32,
            )

        zeros = jnp.zeros((128, hidden), jnp.float32)
        sums.append(lax.fori_loop(0, pl.cdiv(count, GROUP), one_group, zeros))
        own.append(panel_ref[first_ref[0] + tile])
    summed = jnp.concatenate(sums, axis=0)
    neighbour = (root_ref[:, :1] * summed).astype(jnp.bfloat16)
    layer = jnp.concatenate(own, axis=0)
    embedding = (
        jnp.dot(layer, ws_ref[...], preferred_element_type=jnp.float32)
        + jnp.dot(neighbour, wn_ref[...], preferred_element_type=jnp.float32)
        + b_ref[...]
    )
    emb_ref[...] = embedding.astype(emb_ref.dtype)
    cotangent = cot_ref[...]

    @pl.when(step == 0)
    def _():
        grad_ref[...] = jnp.zeros_like(grad_ref)
        bias_ref[...] = jnp.zeros_like(bias_ref)

    grad_ref[...] += lax.dot_general(
        jnp.concatenate([layer, neighbour], axis=1),
        cotangent,
        (((0,), (0,)), ((), ())),
        preferred_element_type=jnp.float32,
    )
    bias_ref[...] += jnp.sum(
        cotangent.astype(jnp.float32).reshape(-1, 8, cotangent.shape[1]), axis=0
    )


def reduce_kernel(
    n_dom, n_feat, g_ref, b_ref, out_ref, bias_ref,
    by_dom, bias_dom, by_feat, bias_feat, send_sem, recv_sem,
):
    dom, feat = lax.axis_index("dom"), lax.axis_index("feat")
    share = g_ref.shape[0] // n_dom

    def dom_at(step):
        return lax.rem(dom + step, n_dom)

    def feat_at(step):
        return lax.rem(feat + step, n_feat)

    def rows(index):
        return pl.ds(pl.multiple_of(index * share, share), share)

    def copy(kind, source, target, step, device_id):
        return pltpu.make_async_remote_copy(
            src_ref=source,
            dst_ref=target,
            send_sem=send_sem.at[kind, step],
            recv_sem=recv_sem.at[kind, step],
            device_id=device_id,
            device_id_type=MESH,
        )

    barrier = pltpu.get_barrier_semaphore()
    for step in range(1, n_dom):
        pl.semaphore_signal(
            barrier, inc=1, device_id=(dom_at(step), feat), device_id_type=MESH
        )
    for step in range(1, n_feat):
        pl.semaphore_signal(
            barrier, inc=1, device_id=(dom, feat_at(step)), device_id_type=MESH
        )
    pl.semaphore_wait(barrier, n_dom + n_feat - 2)

    scatter = []
    for step in range(1, n_dom):
        to = (dom_at(step), feat)
        scatter.append(copy(0, g_ref.at[rows(dom_at(step))], by_dom.at[dom], step, to))
        scatter.append(copy(1, b_ref, bias_dom.at[dom], step, to))
    for each in scatter:
        each.start()
    by_dom[dom] = g_ref[rows(dom), :]
    bias_dom[dom] = b_ref[...]
    for each in scatter:
        each.wait()
    by_feat[feat] = functools.reduce(lambda a, b: a + b, [by_dom[i] for i in range(n_dom)])
    bias_feat[feat] = functools.reduce(
        lambda a, b: a + b, [bias_dom[i] for i in range(n_dom)]
    )

    across = []
    for step in range(1, n_feat):
        to = (dom, feat_at(step))
        across.append(copy(2, by_feat.at[feat], by_feat.at[feat], step, to))
        across.append(copy(3, bias_feat.at[feat], bias_feat.at[feat], step, to))
    for each in across:
        each.start()
    for each in across:
        each.wait()
    out_ref[rows(dom), :] = functools.reduce(
        lambda a, b: a + b, [by_feat[i] for i in range(n_feat)]
    )
    bias_ref[...] = functools.reduce(lambda a, b: a + b, [bias_feat[i] for i in range(n_feat)])

    spread = [
        copy(4, out_ref.at[rows(dom)], out_ref.at[rows(dom)], step, (dom_at(step), feat))
        for step in range(1, n_dom)
    ]
    for each in spread:
        each.start()
    for each in spread:
        each.wait()


def reduce_all(grads, bias, n_dom, n_feat):
    share = grads.shape[0] // n_dom
    width = grads.shape[1]
    steps = max(n_dom, n_feat)
    whole = pl.BlockSpec(memory_space=pltpu.VMEM)
    return pl.pallas_call(
        functools.partial(reduce_kernel, n_dom, n_feat),
        out_shape=(
            jax.ShapeDtypeStruct(grads.shape, jnp.float32),
            jax.ShapeDtypeStruct(bias.shape, jnp.float32),
        ),
        in_specs=[whole] * 2,
        out_specs=(whole, whole),
        scratch_shapes=[
            pltpu.VMEM((n_dom, share, width), jnp.float32),
            pltpu.VMEM((n_dom,) + bias.shape, jnp.float32),
            pltpu.VMEM((n_feat, share, width), jnp.float32),
            pltpu.VMEM((n_feat,) + bias.shape, jnp.float32),
            pltpu.SemaphoreType.DMA((5, steps)),
            pltpu.SemaphoreType.DMA((5, steps)),
        ],
        compiler_params=pltpu.CompilerParams(
            collective_id=2, has_side_effects=True, vmem_limit_bytes=VMEM_LIMIT
        ),
        name="reduce_all",
    )(grads, bias)


def on_device(
    features, w1_self, w1_neigh, b1, w2_self, w2_neigh, b2, col_tiles, edge_weights, cotangent
):
    n_feat = lax.axis_size("feat")
    n_dom = lax.axis_size("dom")
    row_tiles, slots = col_tiles.shape
    panel_tiles = row_tiles * n_feat
    all_tiles = panel_tiles * n_dom
    hidden = w1_self.shape[1]
    occupied = col_tiles >= 0
    relative = jnp.mod(col_tiles - (lax.axis_index("dom") - 1) * panel_tiles, all_tiles)
    relative = jnp.where(occupied, relative, 3 * panel_tiles)
    live = jnp.broadcast_to(
        occupied.astype(jnp.float32).reshape(row_tiles * slots, 1), (row_tiles * slots, 128)
    )
    counts = jnp.sum(occupied.astype(jnp.int32), axis=1)
    first_own = jnp.full(
        (1,), panel_tiles + lax.axis_index("feat") * row_tiles, jnp.int32
    )
    rows = row_tiles * 128
    whole = pl.BlockSpec(memory_space=pltpu.VMEM)
    scalars = pl.BlockSpec(memory_space=pltpu.SMEM)
    anywhere = pl.BlockSpec(memory_space=pl.ANY)
    dma = pltpu.SemaphoreType.DMA

    panel_two, inv_root = pl.pallas_call(
        functools.partial(first_kernel, n_dom, n_feat),
        out_shape=(
            jax.ShapeDtypeStruct((3, n_feat, rows, hidden), jnp.bfloat16),
            jax.ShapeDtypeStruct((rows, 128), jnp.float32),
        ),
        in_specs=[anywhere, scalars, whole, anywhere, whole, whole, whole],
        out_specs=(anywhere, whole),
        scratch_shapes=[
            pltpu.VMEM((3, n_feat) + features.shape, jnp.bfloat16),
            pltpu.VMEM((3 * panel_tiles + 1, w1_self.shape[0], 128), jnp.bfloat16),
            pltpu.VMEM(edge_weights.shape, jnp.bfloat16),
            pltpu.VMEM((rows, hidden), jnp.bfloat16),
            dma,
            dma((PIECES_TWO,)),
            dma((4, n_feat, PIECES_ONE)),
            dma((3, n_feat, PIECES_ONE)),
            dma((4, n_feat, PIECES_TWO)),
            dma((3, n_feat, PIECES_TWO)),
        ],
        compiler_params=pltpu.CompilerParams(
            collective_id=0, has_side_effects=True, vmem_limit_bytes=VMEM_LIMIT
        ),
        name="first_layer",
    )(
        features,
        relative,
        live,
        edge_weights,
        w1_self,
        w1_neigh,
        b1[None],
    )

    def fixed(*shape):
        return pl.BlockSpec(
            shape, lambda r, *_: (0,) * len(shape), pipeline_mode=pl.Buffered(1)
        )

    def by_step(width):
        return pl.BlockSpec((256, width), lambda r, *_: (r, 0))

    panel_two = panel_two.reshape(3 * panel_tiles, 128, hidden)
    embedding, grads, bias = pl.pallas_call(
        second_kernel,
        grid_spec=pltpu.PrefetchScalarGridSpec(
            num_scalar_prefetch=3,
            grid=(row_tiles // 2,),
            in_specs=[
                fixed(3 * panel_tiles, 128, hidden),
                pl.BlockSpec((2, slots, 128, 128), lambda r, *_: (r, 0, 0, 0)),
                by_step(128),
                by_step(hidden),
                fixed(hidden, hidden),
                fixed(hidden, hidden),
                fixed(1, hidden),
            ],
            out_specs=(
                by_step(hidden),
                pl.BlockSpec((2 * hidden, hidden), lambda r, *_: (0, 0)),
                pl.BlockSpec((8, hidden), lambda r, *_: (0, 0)),
            ),
        ),
        out_shape=(
            jax.ShapeDtypeStruct((rows, hidden), jnp.bfloat16),
            jax.ShapeDtypeStruct((2 * hidden, hidden), jnp.float32),
            jax.ShapeDtypeStruct((8, hidden), jnp.float32),
        ),
        compiler_params=pltpu.CompilerParams(vmem_limit_bytes=VMEM_LIMIT),
        name="second_layer",
    )(
        jnp.where(occupied, relative, 0), counts, first_own, panel_two, edge_weights, inv_root, cotangent,
        w2_self, w2_neigh, b2[None],
    )
    grads, bias = reduce_all(grads, bias, n_dom, n_feat)
    return (embedding, grads[:hidden], grads[hidden:], jnp.sum(bias, axis=0))


def solution(mesh):
    placed = (
        P("feat", "dom"),
        P(),
        P(),
        P(),
        P(),
        P(),
        P(),
        P(("dom", "feat"), None),
        P(("dom", "feat"), None, None, None),
        P(("dom", "feat"), None),
    )
    return jax.shard_map(
        on_device,
        mesh=mesh,
        in_specs=placed,
        out_specs=(P(("dom", "feat"), None), P(), P(), P()),
        check_vma=False,
    )
```

time: 229 us -> 211 us (0.921); the launches traced: 233 us -> 211 us
  Pallas kernels: 227 us -> 203 us
    pallas_call x3 -> x1, Pallas kernels: 172 us -> 150 us  [on_device(): pl.pallas_call(functools.partial(first_kernel, n_dom, n_feat), out_shape=...]
    pallas_call x1, Pallas kernels: 29.8 us -> 25.8 us  [on_device(): pl.pallas_call(second_kernel, grid_spec=pltpu.PrefetchScalarGridSpec(num_...]
where the time goes in v2:
time: 211 us
  Pallas kernels  203 us (96%)
  other arithmetic  3.91 us (2%)
  local copies, waits for them, and re-layouts  2.77 us (1%)
    pallas_call x1, Pallas kernels, on_device(): pl.pallas_call(functools.partial(first_kernel, n_dom, n_feat), out_shape=...  150 us
    pallas_call x1, Pallas kernels, reduce_all(): pl.pallas_call(functools.partial(reduce_kernel, n_dom, n_feat), out_shape...  27 us
    pallas_call x1, Pallas kernels, on_device(): pl.pallas_call(second_kernel, grid_spec=pltpu.PrefetchScalarGridSpec(num_...  25.8 us

profile of v2, /device:TPU:1, one launch (start us, length us, event | category | flops | bytes accessed | tf_op | source)
XLA Modules:
  0.0 210.5 jit_solution(2678628782480026941)
XLA Ops:
  0.6 0.7 fusion.2
  1.3 0.1 reshape.14
  1.4 1.9 broadcast_select_fusion
  3.4 0.8 broadcast_in_dim.28.live_ref
  4.2 150.4 %first_layer.1 = (bf16[3,4,2048,256]{3,2,1,0:T(8,128)(2,1)}, f32[2048,128]{1,0:T(8,128)}) custom-call(bf16[32,8192]{1,0:T(8,128)(2,1)} %x_ref.1, s32[16,32]{1,0:T(8,128)} %get-tuple-element.21.where_ref, f32[512,128]{1,0:T(8,128)} %broadcast_in_dim.28.live_ref, bf16[16,32,128,128]{3,2,1,0:T(8,128)(2,1)} %edge_ref.1, bf16[128,256]{1,0:T(8,128)(2,1)} %ws_ref.2, ...), custom_call_target="tpu_custom_call" | custom-call | tf_op jit(solution)/shard_map/first_layer/pallas_call | solution.py:402
  154.6 25.8 %second_layer.1 = (bf16[2048,256]{1,0:T(8,128)(2,1)}, f32[512,256]{1,0:T(8,128)}, f32[8,256]{1,0:T(8,128)}) custom-call(s32[16,32]{1,0:T(8,128)} %get-tuple-element.20.where_ref, s32[16]{0:T(128)} %get-tuple-element.24.count_ref, s32[1]{0:T(128)} %bitcast.first_ref, bf16[192,128,256]{2,1,0:T(8,128)(2,1)} %bitcast.4, bf16[16,32,128,128]{3,2,1,0:T(8,128)(2,1)} %edge_ref.1, ...), custom_call_target="tpu_custom_call" | custom-call | tf_op jit(solution)/shard_map/second_layer/pallas_call | solution.py:445
  180.4 27.0 %reduce_all.1 = (f32[512,256]{1,0:T(8,128)}, f32[8,256]{1,0:T(8,128)}) custom-call(f32[512,256]{1,0:T(8,128)} %get-tuple-element.14.g_ref, f32[8,256]{1,0:T(8,128)} %get-tuple-element.15.b_ref), custom_call_target="tpu_custom_call" | custom-call | tf_op jit(solution)/shard_map/reduce_all/pallas_call | solution.py:354
  207.4 1.9 fusion.4
  209.2 1.3 reduce_sum.19

commit v3 on v2

--- a/solution.py
+++ b/solution.py
@@ -68,6 +68,48 @@
                 device_id_type=MESH,
             )
 
+        half = pieces // 2 if n_feat >= 4 else 0
+        even = lax.rem(dom, 2) == 0
+        far = 2 * lax.rem(dom, 2)
+        relays = (
+            (0, 0, above, (feat == 0) | (feat == n_feat - 2)),
+            (1, n_feat - 1, below, (feat == 1) | (feat == n_feat - 1)),
+        )
+
+        def relayed(block):
+            return (((feat == 0) | (feat == n_feat - 2)) & (block == n_feat - 1)) | (
+                ((feat == 1) | (feat == n_feat - 1)) & (block == 0)
+            )
+
+        def across(block, piece, own, act):
+            for way, outer in ((2, even), (3, jnp.logical_not(even))):
+                if piece < half:
+                    pl.when(jnp.logical_not(outer & relayed(block)))(
+                        lambda way=way: act(copy(way, block, piece, own))
+                    )
+                else:
+                    act(copy(way, block, piece, own))
+
+        def relay_copy(block, target, piece):
+            part = held_ref.at[far, block, rows(piece)]
+            return pltpu.make_async_remote_copy(
+                src_ref=part,
+                dst_ref=part,
+                send_sem=send_sem.at[4, block, piece],
+                recv_sem=recv_sem.at[far, block, piece],
+                device_id=(dom, target),
+                device_id_type=MESH,
+            )
+
+        def relay():
+            for piece in range(half):
+                for _, block, target, there in relays:
+
+                    @pl.when(there)
+                    def _():
+                        arrival(far, block, piece).wait()
+                        relay_copy(block, target, piece).start()
+
         def arrival(slot, block, piece):
             part = held_ref.at[slot, block, rows(piece)]
             return pltpu.make_async_copy(part, part, recv_sem.at[slot, block, piece])
@@ -79,8 +121,7 @@
                 def _():
                     copy(way, feat, piece, True).start()
 
-            copy(2, feat, piece, True).start()
-            copy(3, feat, piece, True).start()
+            across(feat, piece, True, lambda each: each.start())
 
         def streams(step):
             return (
@@ -101,8 +142,7 @@
                             def _():
                                 copy(way, block, piece, False).start()
 
-                            copy(2, block, piece, False).start()
-                            copy(3, block, piece, False).start()
+                            across(block, piece, False, lambda each: each.start())
 
         def finish_sends():
             for piece in range(pieces):
@@ -112,8 +152,14 @@
                     def _():
                         copy(way, feat, piece, True).wait_send()
 
-                copy(2, feat, piece, True).wait_send()
-                copy(3, feat, piece, True).wait_send()
+                across(feat, piece, True, lambda each: each.wait_send())
+                if piece < half:
+                    for _, block, target, there in relays:
+
+                        @pl.when(there)
+                        def _():
+                            relay_copy(block, target, piece).wait_send()
+
                 for step in range(1, n_feat):
                     for way, block, there, onward in streams(step):
 
@@ -123,23 +169,30 @@
                             def _():
                                 copy(way, block, piece, False).wait_send()
 
-                            copy(2, block, piece, False).wait_send()
-                            copy(3, block, piece, False).wait_send()
+                            across(block, piece, False, lambda each: each.wait_send())
 
         def arrive():
             for piece in range(pieces):
                 for block in range(n_feat):
-                    arrival(0, block, piece).wait()
-                    arrival(2, block, piece).wait()
-
-        return send_own, forward, finish_sends, arrive
-
-    send_own, forward, finish_one, arrive = gather(x_ref, panel, PIECES_ONE, send_one, recv_one)
+                    for slot in (0, 2):
+                        passed_on = False
+                        if piece < half:
+                            for _, relay_block, _, there in relays:
+                                if relay_block == block:
+                                    passed_on = there & (far == slot)
+                        pl.when(jnp.logical_not(passed_on))(
+                            lambda slot=slot, block=block: arrival(slot, block, piece).wait()
+                        )
+
+        return send_own, forward, relay, finish_sends, arrive
+
+    send_own, forward, relay, finish_one, arrive = gather(x_ref, panel, PIECES_ONE, send_one, recv_one)
     keep = pltpu.make_async_copy(x_ref, panel.at[1, feat], own_sem)
     for piece in range(PIECES_ONE):
         send_own(piece)
     keep.start()
     forward()
+    relay()
     keep.wait()
     arrive()
 
@@ -201,7 +254,7 @@
         layer_ref[rows, :] = layer.astype(layer_ref.dtype)
         root_ref[rows, :] = jnp.broadcast_to(inv_root, (256, 128))
 
-    send_own, forward, finish_two, arrive = gather(
+    send_own, forward, relay, finish_two, arrive = gather(
         layer_ref, out_ref, PIECES_TWO, send_two, recv_two
     )
     pairs = step_tiles // 2
@@ -212,6 +265,7 @@
     keep = pltpu.make_async_copy(layer_ref, out_ref.at[1, feat], own_sem)
     keep.start()
     forward()
+    relay()
     keep.wait()
     finish_one()
     finish_two()
@@ -414,9 +468,9 @@
             pltpu.VMEM((rows, hidden), jnp.bfloat16),
             dma,
             dma((PIECES_TWO,)),
-            dma((4, n_feat, PIECES_ONE)),
+            dma((5, n_feat, PIECES_ONE)),
             dma((3, n_feat, PIECES_ONE)),
-            dma((4, n_feat, PIECES_TWO)),
+            dma((5, n_feat, PIECES_TWO)),
             dma((3, n_feat, PIECES_TWO)),
         ],
         compiler_params=pltpu.CompilerParams(

time: 211 us -> 193 us (0.915); the launches traced: 211 us -> 190 us
  Pallas kernels: 203 us -> 183 us
    pallas_call x1, Pallas kernels: 150 us -> 135 us  [on_device(): pl.pallas_call(functools.partial(first_kernel, n_dom, n_feat), out_shape=...]
    pallas_call x1, Pallas kernels: 25.8 us -> 20.1 us  [on_device(): pl.pallas_call(second_kernel, grid_spec=pltpu.PrefetchScalarGridSpec(num_...]
where the time goes in v3:
time: 193 us; the launch traced here: 190 us
  Pallas kernels  183 us (95%)
  other arithmetic  3.91 us (2%)
  local copies, waits for them, and re-layouts  2.77 us (1%)
    pallas_call x1, Pallas kernels, on_device(): pl.pallas_call(functools.partial(first_kernel, n_dom, n_feat), out_shape=...  135 us
    pallas_call x1, Pallas kernels, reduce_all(): pl.pallas_call(functools.partial(reduce_kernel, n_dom, n_feat), out_shape...  27.7 us
    pallas_call x1, Pallas kernels, on_device(): pl.pallas_call(second_kernel, grid_spec=pltpu.PrefetchScalarGridSpec(num_...  20.1 us

profile of v3, /device:TPU:1, one launch (start us, length us, event | category | flops | bytes accessed | tf_op | source)
XLA Modules:
  0.0 189.9 jit_solution(1186717941104708316)
XLA Ops:
  0.6 0.7 fusion.2
  1.3 0.1 reshape.14
  1.4 1.9 %broadcast_select_fusion = (s32[16,32]{1,0:T(8,128)}, s32[16,32]{1,0:T(8,128)}, s32[16]{0:T(128)}) fusion(pred[16,32]{1,0:T(8,128)(4,1)S(1)} %get-tuple-element.19, s32[16,32]{1,0:T(8,128)} %param.17, s32[]{:T(128)S(6)} %mul.6), kind=kLoop, calls=%fused_computation.6 | loop fusion | flops 8176 | bytes 6724 | tf_op jit(solution)/shard_map/jit(_where)/select_n | solution.py:527
  3.4 0.8 broadcast_in_dim.28.live_ref
  4.2 134.9 %first_layer.1 = (bf16[3,4,2048,256]{3,2,1,0:T(8,128)(2,1)}, f32[2048,128]{1,0:T(8,128)}) custom-call(bf16[32,8192]{1,0:T(8,128)(2,1)} %x_ref.1, s32[16,32]{1,0:T(8,128)} %get-tuple-element.21.where_ref, f32[512,128]{1,0:T(8,128)} %broadcast_in_dim.28.live_ref, bf16[16,32,128,128]{3,2,1,0:T(8,128)(2,1)} %edge_ref.1, bf16[128,256]{1,0:T(8,128)(2,1)} %ws_ref.2, ...), custom_call_target="tpu_custom_call" | custom-call | tf_op jit(solution)/shard_map/first_layer/pallas_call | solution.py:456
  139.1 20.1 %second_layer.1 = (bf16[2048,256]{1,0:T(8,128)(2,1)}, f32[512,256]{1,0:T(8,128)}, f32[8,256]{1,0:T(8,128)}) custom-call(s32[16,32]{1,0:T(8,128)} %get-tuple-element.20.where_ref, s32[16]{0:T(128)} %get-tuple-element.24.count_ref, s32[1]{0:T(128)} %bitcast.first_ref, bf16[192,128,256]{2,1,0:T(8,128)(2,1)} %bitcast.4, bf16[16,32,128,128]{3,2,1,0:T(8,128)(2,1)} %edge_ref.1, ...), custom_call_target="tpu_custom_call" | custom-call | tf_op jit(solution)/shard_map/second_layer/pallas_call | solution.py:499
  159.1 27.7 %reduce_all.1 = (f32[512,256]{1,0:T(8,128)}, f32[8,256]{1,0:T(8,128)}) custom-call(f32[512,256]{1,0:T(8,128)} %get-tuple-element.14.g_ref, f32[8,256]{1,0:T(8,128)} %get-tuple-element.15.b_ref), custom_call_target="tpu_custom_call" | custom-call | tf_op jit(solution)/shard_map/reduce_all/pallas_call | solution.py:408
  186.8 1.9 fusion.4
  188.7 1.3 reduce_sum.19
